TPU v7x, 32 devices: a whole 2x2x4 slice. The times are simulated.
32 devices in a mesh: seq: 8 (over y, x, core), head: 4 (over z).
Axes of the slice: x: 2, y: 2, z: 4, core: 2. Of those that a mesh axis runs over, the one named last changes fastest.
Arguments:
- queries: bfloat16 [4096, 4096], P(('seq', 'head')), may hold values from -1.796875 to 1.796875
- keys: bfloat16 [4096, 4096], P(('seq', 'head')), may hold values from -1.796875 to 1.796875
- values: bfloat16 [4096, 4096], P(('seq', 'head')), may hold values from -1.796875 to 1.796875
- grad_out: bfloat16 [4096, 4096], P(('seq', 'head')), may hold values from -0.09375 to 0.09375
Outputs:
- grad_q: bfloat16 [4096, 4096], P(('seq', 'head'))
- grad_k: bfloat16 [4096, 4096], P(('seq', 'head'))
- grad_v: bfloat16 [4096, 4096], P(('seq', 'head'))
All inputs are finite; a program needn't handle non-finite values.
Results may differ from a plain program's by a relative error of at most 0.0025.
Values may be sent and summed in bfloat16 or wider, within the bound.
A program may use at most 128 MiB of HBM per device.

v0:
```python
import jax
import jax.numpy as jnp
from jax import lax
from jax.sharding import PartitionSpec as P

DK = 128


def carried_in(value, axis, combine, identity, reverse):
    size, mine = (lax.axis_size(axis), lax.axis_index(axis))
    everything = lax.all_gather(value, axis)
    start = jnp.broadcast_to(jnp.asarray(identity, value.dtype), value.shape)

    def step(k, before):
        at = size - 1 - k if reverse else k
        reached = at > mine if reverse else at < mine
        new = combine(before, everything[at])
        return jnp.where(reached, new, before)

    return lax.fori_loop(0, size, step, start)


def add_pair(earlier, later):
    return earlier + later


def outer_state(left, right):
    return jnp.einsum("chd,che->hde", left, right, preferred_element_type=jnp.float32)


def body(queries, keys, values, grad_out):
    query_rows, key_rows, value_rows, grad_rows = (
        lax.all_to_all(queries, "head", split_axis=1, concat_axis=0, tiled=True),
        lax.all_to_all(keys, "head", split_axis=1, concat_axis=0, tiled=True),
        lax.all_to_all(values, "head", split_axis=1, concat_axis=0, tiled=True),
        lax.all_to_all(grad_out, "head", split_axis=1, concat_axis=0, tiled=True),
    )
    rows = key_rows.shape[0]
    width = key_rows.shape[1]
    heads_here = width // DK
    key_three = key_rows.reshape(rows, heads_here, DK)
    value_three = value_rows.reshape(rows, heads_here, DK)
    key_state = outer_state(key_three, value_three)
    query_three = query_rows.reshape(rows, heads_here, DK)
    grad_three = grad_rows.reshape(rows, heads_here, DK)
    grad_state = outer_state(query_three, grad_three)
    zeros = jnp.zeros_like(key_state)
    prefix = carried_in(key_state, "seq", add_pair, zeros, False)
    suffix = carried_in(grad_state, "seq", add_pair, zeros, True)
    position = lax.iota(jnp.int32, rows)
    causal = position[:, None] >= position[None, :]
    high = lax.Precision.HIGHEST
    query_list = []
    key_list = []
    value_list = []
    for head in range(heads_here):
        query_one = query_three[:, head, :]
        key_one = key_three[:, head, :]
        value_one = value_three[:, head, :]
        grad_one = grad_three[:, head, :]
        weights_a = jnp.where(
            causal, jnp.dot(grad_one, value_one.T, preferred_element_type=jnp.float32), 0.0
        ).astype(jnp.bfloat16)
        weights_b = jnp.where(
            causal, jnp.dot(query_one, key_one.T, preferred_element_type=jnp.float32), 0.0
        ).astype(jnp.bfloat16)
        grad_query = jnp.dot(weights_a, key_one, preferred_element_type=jnp.float32)
        grad_query = grad_query + jnp.dot(
            grad_one.astype(jnp.float32), prefix[head].T, precision=high
        )
        grad_key = jnp.dot(weights_a.T, query_one, preferred_element_type=jnp.float32)
        grad_key = grad_key + jnp.dot(value_one.astype(jnp.float32), suffix[head].T, precision=high)
        grad_value = jnp.dot(weights_b.T, grad_one, preferred_element_type=jnp.float32)
        grad_value = grad_value + jnp.dot(key_one.astype(jnp.float32), suffix[head], precision=high)
        query_list.append(grad_query.astype(jnp.bfloat16))
        key_list.append(grad_key.astype(jnp.bfloat16))
        value_list.append(grad_value.astype(jnp.bfloat16))
    results = (
        jnp.stack(query_list, axis=1).reshape(rows, width),
        jnp.stack(key_list, axis=1).reshape(rows, width),
        jnp.stack(value_list, axis=1).reshape(rows, width),
    )
    out_query, out_key, out_value = (
        lax.all_to_all(results[0], "head", split_axis=0, concat_axis=1, tiled=True),
        lax.all_to_all(results[1], "head", split_axis=0, concat_axis=1, tiled=True),
        lax.all_to_all(results[2], "head", split_axis=0, concat_axis=1, tiled=True),
    )
    return (out_query, out_key, out_value)


def solution(mesh):
    in_specs = (
        P(("seq", "head"), None),
        P(("seq", "head"), None),
        P(("seq", "head"), None),
        P(("seq", "head"), None),
    )
    out_specs = (P(("seq", "head"), None), P(("seq", "head"), None), P(("seq", "head"), None))
    return jax.shard_map(body, mesh=mesh, in_specs=in_specs, out_specs=out_specs, check_vma=False)
```

profile of v0, /device:TPU:0, one launch (start us, length us, event | category | flops | bytes accessed | tf_op | source)
XLA Modules:
  0.0 324.0 jit_solution(5730055158160054674)
XLA Ops:
  7.2 2.4 copy.120
  9.5 6.3 %all-to-all-start.4 = ((bf16[128,4,1024]{0,2,1:T(8,128)(2,1)}), bf16[128,4,1024]{0,2,1:T(8,128)(2,1)S(1)}, u32[]{:S(2)}, u32[]{:S(2)}) async-start(bf16[128,4,1024]{0,2,1:T(8,128)(2,1)} %bitcast.39), calls=%async_computation.4 | async-start | bytes 2097152 | tf_op jit(solution)/shard_map/all_to_all | solution.py:33
  16.9 24.7 %all-to-all-done.4 = bf16[128,4,1024]{0,2,1:T(8,128)(2,1)S(1)} async-done(((bf16[128,4,1024]{0,2,1:T(8,128)(2,1)}), bf16[128,4,1024]{0,2,1:T(8,128)(2,1)S(1)}, u32[]{:S(2)}, u32[]{:S(2)}) %all-to-all-start.4) | async-done | bytes 1048608 | tf_op jit(solution)/shard_map/all_to_all | solution.py:33
  41.6 3.5 %all-to-all-start = ((bf16[128,4,1024]{2,0,1:T(8,128)(2,1)}), bf16[128,4,1024]{2,0,1:T(8,128)(2,1)S(1)}, u32[]{:S(2)}, u32[]{:S(2)}) async-start(bf16[128,4,1024]{2,0,1:T(8,128)(2,1)} %bitcast.445), calls=%async_computation | async-start | bytes 2097152 | tf_op jit(solution)/shard_map/all_to_all | solution.py:36
  48.4 21.9 %all-to-all-done = bf16[128,4,1024]{2,0,1:T(8,128)(2,1)S(1)} async-done(((bf16[128,4,1024]{2,0,1:T(8,128)(2,1)}), bf16[128,4,1024]{2,0,1:T(8,128)(2,1)S(1)}, u32[]{:S(2)}, u32[]{:S(2)}) %all-to-all-start) | async-done | bytes 1048608 | tf_op jit(solution)/shard_map/all_to_all | solution.py:36
  74.0 2.3 copy.107
  76.3 4.3 %all-to-all-start.2 = ((bf16[128,4,1024]{0,2,1:T(8,128)(2,1)}), bf16[128,4,1024]{0,2,1:T(8,128)(2,1)}, u32[]{:S(2)}, u32[]{:S(2)}) async-start(bf16[128,4,1024]{0,2,1:T(8,128)(2,1)} %bitcast.458), calls=%async_computation.2 | async-start | bytes 2097152 | tf_op jit(solution)/shard_map/all_to_all | solution.py:34
  80.6 2.3 copy.356
  82.9 23.0 %all-to-all-done.2 = bf16[128,4,1024]{0,2,1:T(8,128)(2,1)} async-done(((bf16[128,4,1024]{0,2,1:T(8,128)(2,1)}), bf16[128,4,1024]{0,2,1:T(8,128)(2,1)}, u32[]{:S(2)}, u32[]{:S(2)}) %all-to-all-start.2) | async-done | bytes 1048608 | tf_op jit(solution)/shard_map/all_to_all | solution.py:34
  105.9 4.2 %all-to-all-start.1 = ((bf16[128,4,1024]{2,0,1:T(8,128)(2,1)}), bf16[128,4,1024]{2,0,1:T(8,128)(2,1)}, u32[]{:S(2)}, u32[]{:S(2)}) async-start(bf16[128,4,1024]{2,0,1:T(8,128)(2,1)} %bitcast.444), calls=%async_computation.1 | async-start | bytes 2097152 | tf_op jit(solution)/shard_map/all_to_all | solution.py:35
  110.2 3.0 copy.108
  114.6 20.7 %all-to-all-done.1 = bf16[128,4,1024]{2,0,1:T(8,128)(2,1)} async-done(((bf16[128,4,1024]{2,0,1:T(8,128)(2,1)}), bf16[128,4,1024]{2,0,1:T(8,128)(2,1)}, u32[]{:S(2)}, u32[]{:S(2)}) %all-to-all-start.1) | async-done | bytes 1048608 | tf_op jit(solution)/shard_map/all_to_all | solution.py:35
  139.2 1.9 fusion.253
  141.2 1.9 fusion.252
  152.5 10.0 %while.31 = (s32[]{:T(128)}, f32[8,128,128]{2,1,0:T(8,128)S(1)}, s32[]{:T(128)}, f32[8,8,128,128]{3,2,1,0:T(8,128)}, s32[]{:T(128)}, /*index=5*/s32[]{:T(128)}, s32[]{:T(128)}, s32[]{:T(128)}) while((s32[]{:T(128)}, f32[8,128,128]{2,1,0:T(8,128)S(1)}, s32[]{:T(128)}, f32[8,8,128,128]{3,2,1,0:T(8,128)}, s32[]{:T(128)}, ...), condition=%wide.region_3.4_spmd.clone, body=%wide.region_2.3_spmd.clone.sunk | while | flops 393224 | bytes 1573027 | solution.py:20
  170.7 4.4 %all-gather.5.cloned.1.call-done = f32[64,128,128]{2,1,0:T(8,128)} async-done(((f32[8,128,128]{2,1,0:T(8,128)}), f32[64,128,128]{2,1,0:T(8,128)}) %all-gather.5.cloned.1.call-update) | async-done | bytes 4194320 | tf_op jit(solution)/shard_map/all_gather | solution.py:11
  175.1 10.2 %while.30 = (s32[]{:T(128)}, f32[8,128,128]{2,1,0:T(8,128)S(1)}, s32[]{:T(128)}, f32[8,8,128,128]{3,2,1,0:T(8,128)}, s32[]{:T(128)}, /*index=5*/s32[]{:T(128)}) while((s32[]{:T(128)}, f32[8,128,128]{2,1,0:T(8,128)S(1)}, s32[]{:T(128)}, f32[8,8,128,128]{3,2,1,0:T(8,128)}, s32[]{:T(128)}, /*index=5*/s32[]{:T(128)}) %tuple.97), condition=%wide.region_1.2_spmd.clone, body=%wide.region_0.1_spmd.clone.sunk | while | flops 393220 | bytes 1572965 | solution.py:20
  188.6 1.9 convolution_bitcast_fusion.8
  190.5 1.9 convolution_bitcast_fusion.9
  194.3 1.9 convolution_bitcast_fusion.11
  198.2 2.0 convolution_bitcast_fusion.13
  200.1 1.9 convolution_bitcast_fusion.14
  203.1 2.4 fusion.89
  205.4 2.3 fusion.91
  207.7 2.4 fusion.93
  210.1 2.3 fusion.95
  212.4 2.3 fusion.97
  214.7 2.2 fusion.99
  217.0 2.3 fusion.101
  219.3 2.2 fusion.103
  221.5 2.9 copy.141
  224.4 2.3 all_to_all.110
  226.7 4.7 %all-to-all-start.6 = ((bf16[4,128,1024]{2,1,0:T(8,128)(2,1)}), bf16[4,128,1024]{2,1,0:T(8,128)(2,1)}, u32[]{:S(2)}, u32[]{:S(2)}) async-start(bf16[4,128,1024]{2,1,0:T(8,128)(2,1)} %all_to_all.110), calls=%async_computation.6 | async-start | bytes 2097152 | tf_op jit(solution)/shard_map/all_to_all | solution.py:86
  243.1 1.9 convolution_bitcast_fusion.19
  249.5 2.0 fusion.87
  251.5 2.0 fusion.85
  253.5 4.1 %all-to-all-done.6 = bf16[4,128,1024]{2,1,0:T(8,128)(2,1)} async-done(((bf16[4,128,1024]{2,1,0:T(8,128)(2,1)}), bf16[4,128,1024]{2,1,0:T(8,128)(2,1)}, u32[]{:S(2)}, u32[]{:S(2)}) %all-to-all-start.6) | async-done | bytes 1048608 | tf_op jit(solution)/shard_map/all_to_all | solution.py:86
  257.6 3.7 %all-to-all-start.5 = ((bf16[4,128,1024]{2,1,0:T(8,128)(2,1)}), bf16[4,128,1024]{2,1,0:T(8,128)(2,1)S(1)}, u32[]{:S(2)}, u32[]{:S(2)}) async-start(bf16[4,128,1024]{2,1,0:T(8,128)(2,1)} %all_to_all.106), calls=%async_computation.5 | async-start | bytes 2097152 | tf_op jit(solution)/shard_map/all_to_all | solution.py:85
  262.7 2.0 fusion.83
  264.7 2.1 fusion.81
  266.8 2.1 fusion.79
  268.8 2.1 fusion.77
  276.0 10.5 %all-to-all-done.5 = bf16[4,128,1024]{2,1,0:T(8,128)(2,1)S(1)} async-done(((bf16[4,128,1024]{2,1,0:T(8,128)(2,1)}), bf16[4,128,1024]{2,1,0:T(8,128)(2,1)S(1)}, u32[]{:S(2)}, u32[]{:S(2)}) %all-to-all-start.5) | async-done | bytes 1048608 | tf_op jit(solution)/shard_map/all_to_all | solution.py:85
  286.4 3.5 %all-to-all-start.3 = ((bf16[4,128,1024]{2,1,0:T(8,128)(2,1)}), bf16[4,128,1024]{2,1,0:T(8,128)(2,1)S(1)}, u32[]{:S(2)}, u32[]{:S(2)}) async-start(bf16[4,128,1024]{2,1,0:T(8,128)(2,1)} %all_to_all.99), calls=%async_computation.3 | async-start | bytes 2097152 | tf_op jit(solution)/shard_map/all_to_all | solution.py:84
  290.0 2.3 copy.142
  292.2 2.3 copy.145
  295.8 2.3 copy.144
  298.1 17.1 %all-to-all-done.3 = bf16[4,128,1024]{2,1,0:T(8,128)(2,1)S(1)} async-done(((bf16[4,128,1024]{2,1,0:T(8,128)(2,1)}), bf16[4,128,1024]{2,1,0:T(8,128)(2,1)S(1)}, u32[]{:S(2)}, u32[]{:S(2)}) %all-to-all-start.3) | async-done | bytes 1048608 | tf_op jit(solution)/shard_map/all_to_all | solution.py:84
  (146 shorter events, 84.1 us)
Async XLA Ops:
  7.2 8.7 %copy-start.11 = (bf16[128,4096]{1,0:T(8,128)(2,1)S(1)}, bf16[128,4096]{1,0:T(8,128)(2,1)}, u32[]{:S(2)}) copy-start(bf16[128,4096]{1,0:T(8,128)(2,1)} %param.11) | copy-start | bytes 3145732
  9.5 32.0 %all-to-all-start.4 = ((bf16[128,4,1024]{0,2,1:T(8,128)(2,1)}), bf16[128,4,1024]{0,2,1:T(8,128)(2,1)S(1)}, u32[]{:S(2)}, u32[]{:S(2)}) async-start(bf16[128,4,1024]{0,2,1:T(8,128)(2,1)} %bitcast.39), calls=%async_computation.4 | async-start | bytes 2097152 | tf_op jit(solution)/shard_map/all_to_all | solution.py:33
  41.6 28.7 %all-to-all-start = ((bf16[128,4,1024]{2,0,1:T(8,128)(2,1)}), bf16[128,4,1024]{2,0,1:T(8,128)(2,1)S(1)}, u32[]{:S(2)}, u32[]{:S(2)}) async-start(bf16[128,4,1024]{2,0,1:T(8,128)(2,1)} %bitcast.445), calls=%async_computation | async-start | bytes 2097152 | tf_op jit(solution)/shard_map/all_to_all | solution.py:36
  45.1 107.4 %all-gather.7.cloned.1.call-start = ((), (), s32[]{:S(2)}) async-start(), calls=%async_computation.8 | async-start | bytes 4718592 | tf_op jit(solution)/shard_map/all_gather | solution.py:11
  48.4 27.9 %copy-start.2 = (bf16[512,8,128]{0,2,1:T(8,128)(2,1)}, bf16[512,8,128]{0,2,1:T(8,128)(2,1)S(1)}, u32[]{:S(2)}) copy-start(bf16[512,8,128]{0,2,1:T(8,128)(2,1)S(1)} %reshape.52) | copy-start | bytes 3145732
  70.3 1.0 copy-start.4
  76.3 29.5 %all-to-all-start.2 = ((bf16[128,4,1024]{0,2,1:T(8,128)(2,1)}), bf16[128,4,1024]{0,2,1:T(8,128)(2,1)}, u32[]{:S(2)}, u32[]{:S(2)}) async-start(bf16[128,4,1024]{0,2,1:T(8,128)(2,1)} %bitcast.458), calls=%async_computation.2 | async-start | bytes 2097152 | tf_op jit(solution)/shard_map/all_to_all | solution.py:34
  105.9 29.5 %all-to-all-start.1 = ((bf16[128,4,1024]{2,0,1:T(8,128)(2,1)}), bf16[128,4,1024]{2,0,1:T(8,128)(2,1)}, u32[]{:S(2)}, u32[]{:S(2)}) async-start(bf16[128,4,1024]{2,0,1:T(8,128)(2,1)} %bitcast.444), calls=%async_computation.1 | async-start | bytes 2097152 | tf_op jit(solution)/shard_map/all_to_all | solution.py:35
  110.1 65.0 %all-gather.5.cloned.1.call-start = ((), (), s32[]{:S(2)}) async-start(), calls=%async_computation.7 | async-start | bytes 4718592 | tf_op jit(solution)/shard_map/all_gather | solution.py:11
  136.9 1.0 copy-start
  139.2 2.0 copy-start.1
  141.1 6.8 %copy-start.21 = (bf16[512,1,128]{2,1,0:T(2,128)(2,1)}, bf16[512,1,128]{2,1,0:T(2,128)(2,1)S(1)}, u32[]{:S(2)}) copy-start(bf16[512,1,128]{2,1,0:T(2,128)(2,1)S(1)} %get-tuple-element.257) | copy-start | bytes 393220
  141.1 6.8 %copy-start.22 = (bf16[512,1,128]{2,1,0:T(2,128)(2,1)}, bf16[512,1,128]{2,1,0:T(2,128)(2,1)S(1)}, u32[]{:S(2)}) copy-start(bf16[512,1,128]{2,1,0:T(2,128)(2,1)S(1)} %get-tuple-element.256) | copy-start | bytes 393220
  141.1 6.8 %copy-start.24 = (bf16[512,1,128]{2,1,0:T(2,128)(2,1)}, bf16[512,1,128]{2,1,0:T(2,128)(2,1)S(1)}, u32[]{:S(2)}) copy-start(bf16[512,1,128]{2,1,0:T(2,128)(2,1)S(1)} %get-tuple-element.254) | copy-start | bytes 393220
  141.2 6.8 %copy-start.26 = (bf16[512,1,128]{2,1,0:T(2,128)(2,1)}, bf16[512,1,128]{2,1,0:T(2,128)(2,1)S(1)}, u32[]{:S(2)}) copy-start(bf16[512,1,128]{2,1,0:T(2,128)(2,1)S(1)} %get-tuple-element.255) | copy-start | bytes 393220
  141.2 6.8 %copy-start.20 = (bf16[512,1,128]{2,1,0:T(2,128)(2,1)}, bf16[512,1,128]{2,1,0:T(2,128)(2,1)S(1)}, u32[]{:S(2)}) copy-start(bf16[512,1,128]{2,1,0:T(2,128)(2,1)S(1)} %get-tuple-element.258) | copy-start | bytes 393220
  141.2 7.9 %copy-start.17 = (bf16[512,1,128]{2,1,0:T(2,128)(2,1)}, bf16[512,1,128]{2,1,0:T(2,128)(2,1)S(1)}, u32[]{:S(2)}) copy-start(bf16[512,1,128]{2,1,0:T(2,128)(2,1)S(1)} %get-tuple-element.259) | copy-start | bytes 393220
  141.2 9.0 %copy-start.19 = (bf16[512,1,128]{2,1,0:T(2,128)(2,1)}, bf16[512,1,128]{2,1,0:T(2,128)(2,1)S(1)}, u32[]{:S(2)}) copy-start(bf16[512,1,128]{2,1,0:T(2,128)(2,1)S(1)} %get-tuple-element.260) | copy-start | bytes 393220
  141.2 10.1 %copy-start.18 = (bf16[512,1,128]{2,1,0:T(2,128)(2,1)}, bf16[512,1,128]{2,1,0:T(2,128)(2,1)S(1)}, u32[]{:S(2)}) copy-start(bf16[512,1,128]{2,1,0:T(2,128)(2,1)S(1)} %get-tuple-element.261) | copy-start | bytes 393220
  143.1 8.2 %copy-start.29 = (bf16[512,1,128]{2,1,0:T(2,128)(2,1)}, bf16[512,1,128]{2,1,0:T(2,128)(2,1)S(1)}, u32[]{:S(2)}) copy-start(bf16[512,1,128]{2,1,0:T(2,128)(2,1)S(1)} %get-tuple-element.252) | copy-start | bytes 393220
  143.2 8.2 %copy-start.30 = (bf16[512,1,128]{2,1,0:T(2,128)(2,1)}, bf16[512,1,128]{2,1,0:T(2,128)(2,1)S(1)}, u32[]{:S(2)}) copy-start(bf16[512,1,128]{2,1,0:T(2,128)(2,1)S(1)} %get-tuple-element.251) | copy-start | bytes 393220
  143.2 8.2 %copy-start.27 = (bf16[512,1,128]{2,1,0:T(2,128)(2,1)}, bf16[512,1,128]{2,1,0:T(2,128)(2,1)S(1)}, u32[]{:S(2)}) copy-start(bf16[512,1,128]{2,1,0:T(2,128)(2,1)S(1)} %get-tuple-element.253) | copy-start | bytes 393220
  143.2 8.1 %copy-start.31 = (bf16[512,1,128]{2,1,0:T(2,128)(2,1)}, bf16[512,1,128]{2,1,0:T(2,128)(2,1)S(1)}, u32[]{:S(2)}) copy-start(bf16[512,1,128]{2,1,0:T(2,128)(2,1)S(1)} %get-tuple-element.250) | copy-start | bytes 393220
  143.2 8.1 %copy-start.32 = (bf16[512,1,128]{2,1,0:T(2,128)(2,1)}, bf16[512,1,128]{2,1,0:T(2,128)(2,1)S(1)}, u32[]{:S(2)}) copy-start(bf16[512,1,128]{2,1,0:T(2,128)(2,1)S(1)} %get-tuple-element.249) | copy-start | bytes 393220
  143.2 8.1 %copy-start.33 = (bf16[512,1,128]{2,1,0:T(2,128)(2,1)}, bf16[512,1,128]{2,1,0:T(2,128)(2,1)S(1)}, u32[]{:S(2)}) copy-start(bf16[512,1,128]{2,1,0:T(2,128)(2,1)S(1)} %get-tuple-element.248) | copy-start | bytes 393220
  143.2 8.1 %copy-start.34 = (bf16[512,1,128]{2,1,0:T(2,128)(2,1)}, bf16[512,1,128]{2,1,0:T(2,128)(2,1)S(1)}, u32[]{:S(2)}) copy-start(bf16[512,1,128]{2,1,0:T(2,128)(2,1)S(1)} %get-tuple-element.247) | copy-start | bytes 393220
  143.2 8.1 %copy-start.35 = (bf16[512,1,128]{2,1,0:T(2,128)(2,1)}, bf16[512,1,128]{2,1,0:T(2,128)(2,1)S(1)}, u32[]{:S(2)}) copy-start(bf16[512,1,128]{2,1,0:T(2,128)(2,1)S(1)} %get-tuple-element.246) | copy-start | bytes 393220
  185.3 16.8 %copy-start.28 = (bf16[512,1,128]{2,1,0:T(2,128)(2,1)S(1)}, bf16[512,1,128]{2,1,0:T(2,128)(2,1)}, u32[]{:S(2)}) copy-start(bf16[512,1,128]{2,1,0:T(2,128)(2,1)} %copy-done.27) | copy-start | bytes 393220
  185.3 17.8 %copy-start.3 = (bf16[512,8,128]{0,2,1:T(8,128)(2,1)S(1)}, bf16[512,8,128]{0,2,1:T(8,128)(2,1)}, u32[]{:S(2)}) copy-start(bf16[512,8,128]{0,2,1:T(8,128)(2,1)} %copy-done.2) | copy-start | bytes 3145732
  203.1 11.7 %copy-start.23 = (bf16[512,1,128]{2,1,0:T(2,128)(2,1)S(1)}, bf16[512,1,128]{2,1,0:T(2,128)(2,1)}, u32[]{:S(2)}) copy-start(bf16[512,1,128]{2,1,0:T(2,128)(2,1)} %copy-done.22) | copy-start | bytes 393220
  207.7 11.5 %copy-start.25 = (bf16[512,1,128]{2,1,0:T(2,128)(2,1)S(1)}, bf16[512,1,128]{2,1,0:T(2,128)(2,1)}, u32[]{:S(2)}) copy-start(bf16[512,1,128]{2,1,0:T(2,128)(2,1)} %copy-done.24) | copy-start | bytes 393220
  226.7 11.8 %copy-start.7 = (bf16[512,512]{1,0:T(8,128)(2,1)S(1)}, bf16[512,512]{1,0:T(8,128)(2,1)}, u32[]{:S(2)}) copy-start(bf16[512,512]{1,0:T(8,128)(2,1)} %fusion.6) | copy-start | bytes 1572868
  226.7 31.0 %all-to-all-start.6 = ((bf16[4,128,1024]{2,1,0:T(8,128)(2,1)}), bf16[4,128,1024]{2,1,0:T(8,128)(2,1)}, u32[]{:S(2)}, u32[]{:S(2)}) async-start(bf16[4,128,1024]{2,1,0:T(8,128)(2,1)} %all_to_all.110), calls=%async_computation.6 | async-start | bytes 2097152 | tf_op jit(solution)/shard_map/all_to_all | solution.py:86
  231.4 6.2 %copy-start.10 = (bf16[512,512]{1,0:T(8,128)(2,1)S(1)}, bf16[512,512]{1,0:T(8,128)(2,1)}, u32[]{:S(2)}) copy-start(bf16[512,512]{1,0:T(8,128)(2,1)} %fusion.4) | copy-start | bytes 1572868
  231.4 6.2 %copy-start.16 = (f32[512,128]{1,0:T(8,128)S(1)}, f32[512,128]{1,0:T(8,128)}, u32[]{:S(2)}) copy-start(f32[512,128]{1,0:T(8,128)} %convolution_bitcast_fusion.11) | copy-start | bytes 786436
  231.4 6.6 %copy-start.9 = (bf16[512,512]{1,0:T(8,128)(2,1)S(1)}, bf16[512,512]{1,0:T(8,128)(2,1)}, u32[]{:S(2)}) copy-start(bf16[512,512]{1,0:T(8,128)(2,1)} %fusion.5) | copy-start | bytes 1572868
  231.4 6.6 %copy-start.15 = (f32[512,128]{1,0:T(8,128)S(1)}, f32[512,128]{1,0:T(8,128)}, u32[]{:S(2)}) copy-start(f32[512,128]{1,0:T(8,128)} %convolution_bitcast_fusion.10) | copy-start | bytes 786436
  231.4 7.0 %copy-start.14 = (f32[512,128]{1,0:T(8,128)S(1)}, f32[512,128]{1,0:T(8,128)}, u32[]{:S(2)}) copy-start(f32[512,128]{1,0:T(8,128)} %convolution_bitcast_fusion.9) | copy-start | bytes 786436
  231.4 7.4 %copy-start.5 = (bf16[512,512]{1,0:T(8,128)(2,1)S(1)}, bf16[512,512]{1,0:T(8,128)(2,1)}, u32[]{:S(2)}) copy-start(bf16[512,512]{1,0:T(8,128)(2,1)} %fusion.7) | copy-start | bytes 1572868
  231.4 7.4 %copy-start.13 = (f32[512,128]{1,0:T(8,128)S(1)}, f32[512,128]{1,0:T(8,128)}, u32[]{:S(2)}) copy-start(f32[512,128]{1,0:T(8,128)} %convolution_bitcast_fusion.8) | copy-start | bytes 786436
  251.5 20.4 %copy-start.6 = (bf16[512,512]{1,0:T(8,128)(2,1)S(1)}, bf16[512,512]{1,0:T(8,128)(2,1)}, u32[]{:S(2)}) copy-start(bf16[512,512]{1,0:T(8,128)(2,1)} %fusion.7) | copy-start | bytes 1572868
  257.6 28.8 %all-to-all-start.5 = ((bf16[4,128,1024]{2,1,0:T(8,128)(2,1)}), bf16[4,128,1024]{2,1,0:T(8,128)(2,1)S(1)}, u32[]{:S(2)}, u32[]{:S(2)}) async-start(bf16[4,128,1024]{2,1,0:T(8,128)(2,1)} %all_to_all.106), calls=%async_computation.5 | async-start | bytes 2097152 | tf_op jit(solution)/shard_map/all_to_all | solution.py:85
  261.4 9.5 %copy-start.8 = (bf16[512,512]{1,0:T(8,128)(2,1)S(1)}, bf16[512,512]{1,0:T(8,128)(2,1)}, u32[]{:S(2)}) copy-start(bf16[512,512]{1,0:T(8,128)(2,1)} %fusion.6) | copy-start | bytes 1572868
  261.4 9.5 %copy-start.12 = (f32[512,128]{1,0:T(8,128)S(1)}, f32[512,128]{1,0:T(8,128)}, u32[]{:S(2)}) copy-start(f32[512,128]{1,0:T(8,128)} %convolution_bitcast_fusion.17) | copy-start | bytes 786436
  286.4 28.7 %all-to-all-start.3 = ((bf16[4,128,1024]{2,1,0:T(8,128)(2,1)}), bf16[4,128,1024]{2,1,0:T(8,128)(2,1)S(1)}, u32[]{:S(2)}, u32[]{:S(2)}) async-start(bf16[4,128,1024]{2,1,0:T(8,128)(2,1)} %all_to_all.99), calls=%async_computation.3 | async-start | bytes 2097152 | tf_op jit(solution)/shard_map/all_to_all | solution.py:84
Sparse Core Ops, SparseCore 0:
  74.2 35.8 all-gather.6
  139.3 35.8 all-gather.4
where the time goes:
time: 327 us; the launch traced here: 324 us
  waiting for transfers between devices  126 us (39%)
  matrix products  87.4 us (27%)
  local copies, waits for them, and re-layouts  45 us (14%)
  starting transfers between devices  30.4 us (9%)
  other arithmetic  19.6 us (6%)
  between operations  14.6 us (4%)
    all_to_all x1, waiting for transfers between devices, body(): lax.all_to_all(queries, 'head', split_axis=1, concat_axis=0, tiled=True)  24.7 us
    all_to_all x1, waiting for transfers between devices, body(): lax.all_to_all(keys, 'head', split_axis=1, concat_axis=0, tiled=True)  23 us
    all_to_all x1, waiting for transfers between devices, body(): lax.all_to_all(grad_out, 'head', split_axis=1, concat_axis=0, tiled=True)  21.9 us
    all_to_all x1, waiting for transfers between devices, body(): lax.all_to_all(values, 'head', split_axis=1, concat_axis=0, tiled=True)  20.7 us
    select_n x16, other arithmetic, step(): return jnp.where(reached, new, before)  19.6 us
    dot_general x8, matrix products, body(): jnp.dot(weights_b.T, grad_one, preferred_element_type=jnp.float32)  18.4 us
    all_to_all x1, waiting for transfers between devices, body(): lax.all_to_all(results[0], 'head', split_axis=0, concat_axis=1, tiled=True)  17.1 us
    unnamed x79, local copies, waits for them, and re-layouts  15.5 us
  transfers between devices with their start and end apart: 9, of which 8 were waited for; matrix products, arithmetic and copies ran while one was open for 28% of the time, Pallas kernels for 0%

commit v1 on v0

v1 whole, which is shorter than its diff:
```python
import functools

import jax
import jax.numpy as jnp
from jax import lax
from jax.experimental import pallas as pl
from jax.experimental.pallas import tpu as pltpu
from jax.sharding import PartitionSpec as P

DK = 128
PIECE = 1
MESH = pl.DeviceIdType.MESH
NT = (((1,), (1,)), ((), ()))
TN = (((0,), (0,)), ((), ()))
NN = (((1,), (0,)), ((), ()))


def dot(left, right, dims):
    return lax.dot_general(left, right, dims, preferred_element_type=jnp.float32)


def enc(x):
    return (x * jnp.abs(x) * (x * x)).astype(jnp.bfloat16)


def dec(y):
    y = y.astype(jnp.float32)
    root = jnp.sqrt(jnp.sqrt(jnp.abs(y)))
    return jnp.where(y < 0, -root, root)


def split(x):
    high = x.astype(jnp.bfloat16)
    return high, (x - high.astype(jnp.float32)).astype(jnp.bfloat16)


def kernel(
    ns, nz, q, k, v, o, gq, gk, gv,
    base, s_right, r_right, s_left, r_left, own, total, carried, s_seq, r_seq, p_left, p_right, r_back,
    right_s, right_r, left_s, left_r, seq_s, seq_r, back_left, back_right, back_r,
):
    n, z = lax.axis_index("seq"), lax.axis_index("head")
    rounds = ns.bit_length() - 1
    group = base.shape[1] // nz
    pieces = r_right.shape[1]
    first, last = z == 0, z == nz - 1
    gathered = nz - 1

    def later_bit(r):
        return lax.rem(lax.div(n, 1 << r), 2)

    def partner(r):
        return n + (1 - 2 * later_bit(r)) * (1 << r)

    def remote(src, dst, send, recv, where):
        return pltpu.make_async_remote_copy(
            src_ref=src, dst_ref=dst, send_sem=send, recv_sem=recv, device_id=where, device_id_type=MESH
        )

    def go_right(g, c):
        return remote(s_right.at[g, c], r_right.at[g, c], right_s.at[g, c], right_r.at[g, c], {"head": z + 1})

    def go_left(g, c):
        return remote(s_left.at[g, c], r_left.at[g, c], left_s.at[g, c], left_r.at[g, c], {"head": z - 1})

    def go_seq(r, c):
        return remote(s_seq.at[r, c], r_seq.at[r, c], seq_s.at[r, c], seq_r.at[r, c], {"seq": partner(r)})

    def back_to_left(src, g, c):
        return remote(src, r_back.at[g, c], back_left.at[g, c], back_r.at[g, c], {"head": z - 1})

    def back_to_right(src, g, c):
        return remote(src, r_back.at[g, c], back_right.at[g, c], back_r.at[g, c], {"head": z + 1})

    barrier = pltpu.get_barrier_semaphore()

    @pl.when(z > 0)
    def _():
        pl.semaphore_signal(barrier, inc=1, device_id={"head": z - 1}, device_id_type=MESH)

    @pl.when(z < nz - 1)
    def _():
        pl.semaphore_signal(barrier, inc=1, device_id={"head": z + 1}, device_id_type=MESH)

    for r in range(rounds):
        pl.semaphore_signal(barrier, inc=1, device_id={"seq": partner(r)}, device_id_type=MESH)

    @pl.when(first)
    def _():
        r_right[...] = jnp.zeros_like(r_right)

    @pl.when(last)
    def _():
        r_left[...] = jnp.zeros_like(r_left)

    r_back[z] = jnp.zeros(r_back.shape[1:], r_back.dtype)

    neighbours = (z > 0).astype(jnp.int32) + (z < nz - 1).astype(jnp.int32)
    pl.semaphore_wait(barrier, rounds + neighbours)

    def block(ref, h):
        return ref[:, pl.ds(pl.multiple_of(h * DK, DK), DK)]

    def states(h):
        return dot(block(k, h), block(v, h), TN), dot(block(q, h), block(o, h), TN)

    def right_stage(g, c):
        @pl.when(z > 0)
        def _():
            go_right(g, c).wait_recv()

        for j in range(PIECE):
            h = g * group + c * PIECE + j
            key_state, grad_state = states(h)
            before_key, before_grad = dec(r_right[g, c, j]), dec(r_right[g, c, PIECE + j])
            upto_key, upto_grad = before_key + key_state, before_grad + grad_state
            s_right[g, c, j] = enc(upto_key)
            s_right[g, c, PIECE + j] = enc(upto_grad)
            base[0, h] = before_key
            base[1, h] = -upto_grad
        go_right(g, c).start()

    def left_stage(g, c):
        @pl.when(z < nz - 1)
        def _():
            go_left(g, c).wait_recv()

        for j in range(PIECE):
            h = g * group + c * PIECE + j
            key_state, grad_state = states(h)
            after_key, after_grad = dec(r_left[g, c, j]), dec(r_left[g, c, PIECE + j])
            from_key, from_grad = after_key + key_state, after_grad + grad_state
            s_left[g, c, j] = enc(from_key)
            s_left[g, c, PIECE + j] = enc(from_grad)
            base[0, h] = -from_key
            base[1, h] = after_grad
        go_left(g, c).start()

    def owner_stage(c):
        @pl.when(z > 0)
        def _():
            go_right(z, c).wait_recv()

        @pl.when(z < nz - 1)
        def _():
            go_left(z, c).wait_recv()

        for j in range(PIECE):
            h, i = z * group + c * PIECE + j, c * PIECE + j
            key_state, grad_state = states(h)
            before_key, after_grad = dec(r_right[z, c, j]), dec(r_left[z, c, PIECE + j])
            base[0, h] = before_key
            base[1, h] = after_grad
            sums = (
                before_key + key_state + dec(r_left[z, c, j]),
                dec(r_right[z, c, PIECE + j]) + grad_state + after_grad,
            )
            for s in range(2):
                own[s, i] = sums[s]
                total[s, i] = sums[s]
                carried[s, i] = jnp.zeros((DK, DK), jnp.float32)
                s_seq[0, c, s * PIECE + j] = enc(sums[s])
        go_seq(0, c).start()

    def seq_stage(r, c):
        go_seq(r - 1, c).wait_recv()
        partner_earlier = later_bit(r - 1).astype(jnp.float32)
        for j in range(PIECE):
            h, i = z * group + c * PIECE + j, c * PIECE + j
            got_key, got_grad = dec(r_seq[r - 1, c, j]), dec(r_seq[r - 1, c, PIECE + j])
            new_key = carried[0, i] + got_key * partner_earlier
            new_grad = carried[1, i] + got_grad * (1.0 - partner_earlier)
            if r < rounds:
                carried[0, i] = new_key
                carried[1, i] = new_grad
                total_key, total_grad = total[0, i] + got_key, total[1, i] + got_grad
                total[0, i] = total_key
                total[1, i] = total_grad
                s_seq[r, c, j] = enc(total_key)
                s_seq[r, c, PIECE + j] = enc(total_grad)
            else:
                base[0, h] += new_key
                base[1, h] += new_grad
                p_left[c, j] = enc(new_key)
                p_left[c, PIECE + j] = enc(new_grad + own[1, i])
                p_right[c, j] = enc(new_key + own[0, i])
                p_right[c, PIECE + j] = enc(new_grad)
        if r < rounds:
            go_seq(r, c).start()
        else:
            @pl.when(z > 0)
            def _():
                back_to_left(p_left.at[c], z, c).start()

            @pl.when(z < nz - 1)
            def _():
                back_to_right(p_right.at[c], z, c).start()

    def relay_left(g, c):
        back_to_left(r_back.at[g, c], g, c).wait_recv()

        @pl.when(z > 0)
        def _():
            back_to_left(r_back.at[g, c], g, c).start()

    def relay_right(g, c):
        back_to_right(r_back.at[g, c], g, c).wait_recv()

        @pl.when(z < nz - 1)
        def _():
            back_to_right(r_back.at[g, c], g, c).start()

    rows = q.shape[0]
    causal = lax.broadcasted_iota(jnp.int32, (rows, rows), 0) >= lax.broadcasted_iota(jnp.int32, (rows, rows), 1)

    def finish(g, c):
        for j in range(PIECE):
            h = g * group + c * PIECE + j
            qh, kh, vh, oh = block(q, h), block(k, h), block(v, h), block(o, h)
            prefix_high, prefix_low = split(base[0, h] + dec(r_back[g, c, j]))
            suffix_high, suffix_low = split(base[1, h] + dec(r_back[g, c, PIECE + j]))
            weights_a = jnp.where(causal, dot(oh, vh, NT), 0.0).astype(jnp.bfloat16)
            weights_b = jnp.where(causal, dot(qh, kh, NT), 0.0).astype(jnp.bfloat16)
            grad_q = dot(weights_a, kh, NN) + dot(oh, prefix_high, NT) + dot(oh, prefix_low, NT)
            grad_k = dot(weights_a, qh, TN) + dot(vh, suffix_high, NT) + dot(vh, suffix_low, NT)
            grad_v = dot(weights_b, oh, TN) + dot(kh, suffix_high, NN) + dot(kh, suffix_low, NN)
            columns = pl.ds(pl.multiple_of(h * DK, DK), DK)
            gq[:, columns] = grad_q.astype(jnp.bfloat16)
            gk[:, columns] = grad_k.astype(jnp.bfloat16)
            gv[:, columns] = grad_v.astype(jnp.bfloat16)

    def valid(c):
        return (c >= 0) & (c < pieces)

    def step(t, carry):
        for g in range(nz):
            cl = t - (gathered + rounds) - (g - z)

            @pl.when((g > z) & valid(cl))
            def _():
                relay_left(g, cl)

            cr = t - (gathered + rounds) - (z - g)

            @pl.when((g < z) & valid(cr))
            def _():
                relay_right(g, cr)

        for r in reversed(range(1, rounds + 1)):
            cs = t - gathered - r

            @pl.when(valid(cs))
            def _():
                seq_stage(r, cs)

        co = t - gathered

        @pl.when(valid(co))
        def _():
            owner_stage(co)

        c_right, c_left = t - z, t - (nz - 1 - z)
        for g in range(nz):
            far = nz - 1 - g

            @pl.when((far > z) & valid(c_right))
            def _():
                right_stage(far, c_right)

            @pl.when((g < z) & valid(c_left))
            def _():
                left_stage(g, c_left)

        cf = t - (2 * gathered + rounds)

        @pl.when(valid(cf))
        def _():
            lax.fori_loop(0, nz, lambda g, u: (finish(g, cf), u)[1], 0)

        return carry

    lax.fori_loop(0, pieces + 2 * gathered + rounds, step, 0)

    def drain(c, carry):
        for g in range(nz):
            @pl.when(g > z)
            def _():
                go_right(g, c).wait_send()

            @pl.when(g < z)
            def _():
                go_left(g, c).wait_send()

            @pl.when((g >= z) & (z > 0))
            def _():
                back_to_left(r_back.at[g, c], g, c).wait_send()

            @pl.when((g <= z) & (z < nz - 1))
            def _():
                back_to_right(r_back.at[g, c], g, c).wait_send()

        for r in range(rounds):
            go_seq(r, c).wait_send()
        return carry

    lax.fori_loop(0, pieces, drain, 0)


def body(ns, nz, queries, keys, values, grad_out):
    heads = queries.shape[1] // DK
    group = heads // nz
    pieces = group // PIECE
    rounds = ns.bit_length() - 1
    moved = (pieces, 2 * PIECE, DK, DK)

    def bf(*lead):
        return pltpu.VMEM(lead + moved, jnp.bfloat16)

    def f32(count):
        return pltpu.VMEM((2, count, DK, DK), jnp.float32)

    by_group = pltpu.SemaphoreType.DMA((nz, pieces))
    by_round = pltpu.SemaphoreType.DMA((rounds, pieces))
    return pl.pallas_call(
        functools.partial(kernel, ns, nz),
        out_shape=[jax.ShapeDtypeStruct(queries.shape, jnp.bfloat16)] * 3,
        in_specs=[pl.BlockSpec(memory_space=pltpu.VMEM)] * 4,
        out_specs=[pl.BlockSpec(memory_space=pltpu.VMEM)] * 3,
        scratch_shapes=[
            f32(heads), bf(nz), bf(nz), bf(nz), bf(nz), f32(group), f32(group), f32(group),
            bf(rounds), bf(rounds), bf(), bf(), bf(nz),
            by_group, by_group, by_group, by_group, by_round, by_round, by_group, by_group, by_group,
        ],
        compiler_params=pltpu.CompilerParams(
            collective_id=0, has_side_effects=True, vmem_limit_bytes=48 * 1024 * 1024
        ),
    )(queries, keys, values, grad_out)


def solution(mesh):
    ns, nz = mesh.shape["seq"], mesh.shape["head"]
    spec = P(("seq", "head"), None)
    return jax.shard_map(
        functools.partial(body, ns, nz), mesh=mesh, in_specs=(spec,) * 4, out_specs=(spec,) * 3, check_vma=False
    )
```

time: 327 us -> 86.9 us (0.27)
  waiting for transfers between devices: 126 us -> 0 us
  matrix products: 87.4 us -> 0 us
  Pallas kernels: 0 us -> 80.7 us
  local copies, waits for them, and re-layouts: 45 us -> 5.35 us
  starting transfers between devices: 30.4 us -> 0 us
  other arithmetic: 19.6 us -> 0 us
  between operations: 14.6 us -> 0.65 us
    all_to_all x7 -> x0, waiting for transfers between devices: 122 us -> none  [the longest x1 24.7 us: body(): lax.all_to_all(queries, 'head', split_axis=1, concat_axis=0, tiled=True)]
    dot_general x58 -> x0, matrix products: 87.4 us -> none  [the longest x8 18.4 us: body(): jnp.dot(weights_b.T, grad_one, preferred_element_type=jnp.float32)]
    pallas_call x0 -> x1, Pallas kernels: none -> 80.7 us  [body(): pl.pallas_call(functools.partial(kernel, ns, nz), out_shape=[jax.ShapeDty...]
    all_to_all x7 -> x0, starting transfers between devices: 30.3 us -> none  [the longest x1 6.32 us: body(): lax.all_to_all(queries, 'head', split_axis=1, concat_axis=0, tiled=True)]
    select_n x16 -> x0, other arithmetic: 19.6 us -> none  [step(): return jnp.where(reached, new, before)]
    all_to_all x10 -> x0, local copies, waits for them, and re-layouts: 17.2 us -> none  [the longest x2 4.56 us: body(): lax.all_to_all(results[2], 'head', split_axis=0, concat_axis=1, tiled=True)]
    unnamed x79 -> x7, local copies, waits for them, and re-layouts: 15.5 us -> 5.35 us
    another operation x3 -> x0, local copies, waits for them, and re-layouts: 5.46 us -> none  [the longest x1 2.87 us: body(): jnp.stack(value_list, axis=1).reshape(rows, width)]
  transfers between devices with their start and end apart: 9 -> 0, of which waited for: 8 -> 0; matrix products, arithmetic and copies ran while one was open for 28% -> 0% of each run, Pallas kernels for 0% -> 0%
where the time goes in v1:
time: 86.9 us; the launch traced here: 86.7 us
  Pallas kernels  80.7 us (93%)
  local copies, waits for them, and re-layouts  5.35 us (6%)
    pallas_call x1, Pallas kernels, body(): pl.pallas_call(functools.partial(kernel, ns, nz), out_shape=[jax.ShapeDty...  80.7 us
    unnamed x7, local copies, waits for them, and re-layouts  5.35 us

profile of v1, /device:TPU:0, one launch (start us, length us, event | category | flops | bytes accessed | tf_op | source)
XLA Modules:
  0.0 86.7 jit_solution(16593451668011908672)
XLA Ops:
  0.6 0.0 copy-start
  0.6 1.2 %copy-done = bf16[128,4096]{1,0:T(8,128)(2,1)S(1)} copy-done((bf16[128,4096]{1,0:T(8,128)(2,1)S(1)}, bf16[128,4096]{1,0:T(8,128)(2,1)}, u32[]{:S(2)}) %copy-start) | copy-done | bytes 1048600
  1.9 0.0 copy-start.1
  1.9 1.2 %copy-done.1 = bf16[128,4096]{1,0:T(8,128)(2,1)S(1)} copy-done((bf16[128,4096]{1,0:T(8,128)(2,1)S(1)}, bf16[128,4096]{1,0:T(8,128)(2,1)}, u32[]{:S(2)}) %copy-start.1) | copy-done | bytes 1048600
  3.1 80.7 %shard_map.67 = (bf16[128,4096]{1,0:T(8,128)(2,1)S(1)}, bf16[128,4096]{1,0:T(8,128)(2,1)S(1)}, bf16[128,4096]{1,0:T(8,128)(2,1)S(1)}) custom-call(bf16[128,4096]{1,0:T(8,128)(2,1)S(1)} %copy-done, bf16[128,4096]{1,0:T(8,128)(2,1)S(1)} %copy-done.1, bf16[128,4096]{1,0:T(8,128)(2,1)} %v.1, bf16[128,4096]{1,0:T(8,128)(2,1)} %o.1), custom_call_target="tpu_custom_call" | custom-call | tf_op jit(solution)/shard_map/pallas_call | solution.py:324
  83.7 1.0 %copy.10 = bf16[128,4096]{1,0:T(8,128)(2,1)} copy(bf16[128,4096]{1,0:T(8,128)(2,1)S(1)} %get-tuple-element.6) | data formatting | bytes 2097152
  84.7 1.0 %copy.11 = bf16[128,4096]{1,0:T(8,128)(2,1)} copy(bf16[128,4096]{1,0:T(8,128)(2,1)S(1)} %get-tuple-element.7) | data formatting | bytes 2097152
  85.7 1.0 %copy.12 = bf16[128,4096]{1,0:T(8,128)(2,1)} copy(bf16[128,4096]{1,0:T(8,128)(2,1)S(1)} %get-tuple-element.8) | data formatting | bytes 2097152
Async XLA Ops:
  0.6 1.2 %copy-start = (bf16[128,4096]{1,0:T(8,128)(2,1)S(1)}, bf16[128,4096]{1,0:T(8,128)(2,1)}, u32[]{:S(2)}) copy-start(bf16[128,4096]{1,0:T(8,128)(2,1)} %q.1) | copy-start | bytes 3145732
  1.9 1.2 %copy-start.1 = (bf16[128,4096]{1,0:T(8,128)(2,1)S(1)}, bf16[128,4096]{1,0:T(8,128)(2,1)}, u32[]{:S(2)}) copy-start(bf16[128,4096]{1,0:T(8,128)(2,1)} %k.1) | copy-start | bytes 3145732

commit v2 on v1

v2 whole, which is shorter than its diff:
```python
import functools

import jax
import jax.numpy as jnp
from jax import lax
from jax.experimental import pallas as pl
from jax.experimental.pallas import tpu as pltpu
from jax.sharding import PartitionSpec as P

DK = 128
PIECE = 1
SKEW = 3
MESH = pl.DeviceIdType.MESH
NT = (((1,), (1,)), ((), ()))
TN = (((0,), (0,)), ((), ()))
NN = (((1,), (0,)), ((), ()))


def dot(left, right, dims):
    return lax.dot_general(left, right, dims, preferred_element_type=jnp.float32)


def enc(x):
    return (x * jnp.abs(x) * (x * x)).astype(jnp.bfloat16)


def dec(y):
    y = y.astype(jnp.float32)
    root = jnp.sqrt(jnp.sqrt(jnp.abs(y)))
    return jnp.where(y < 0, -root, root)


def split(x):
    high = x.astype(jnp.bfloat16)
    return high, (x - high.astype(jnp.float32)).astype(jnp.bfloat16)


def kernel(
    ns, nz, q, k, v, o, gq, gk, gv,
    base, s_right, r_right, s_left, r_left, own, total, carried, s_seq, r_seq, result, r_back,
    right_s, right_r, left_s, left_r, seq_s, seq_r, back_s, back_r,
):
    n, z = lax.axis_index("seq"), lax.axis_index("head")
    rounds = ns.bit_length() - 1
    group = base.shape[1] // 2
    mine = (z == nz - 1).astype(jnp.int32)
    pieces = r_right.shape[0]
    first, last = z == 0, z == nz - 1
    gathered = nz - 1

    def later_bit(r):
        return lax.rem(lax.div(n, 1 << r), 2)

    def partner(r):
        return n + (1 - 2 * later_bit(r)) * (1 << r)

    def remote(src, dst, send, recv, where):
        return pltpu.make_async_remote_copy(
            src_ref=src, dst_ref=dst, send_sem=send, recv_sem=recv, device_id=where, device_id_type=MESH
        )

    def go_right(c):
        return remote(s_right.at[c], r_right.at[c], right_s.at[c], right_r.at[c], {"head": z + 1})

    def go_left(c):
        return remote(s_left.at[c], r_left.at[c], left_s.at[c], left_r.at[c], {"head": z - 1})

    def go_seq(r, c):
        return remote(s_seq.at[r, c], r_seq.at[r, c], seq_s.at[r, c], seq_r.at[r, c], {"seq": partner(r)})

    def back_to_left(src, c):
        return remote(src, r_back.at[1, c], back_s.at[1, c], back_r.at[1, c], {"head": z - 1})

    def back_to_right(src, c):
        return remote(src, r_back.at[0, c], back_s.at[0, c], back_r.at[0, c], {"head": z + 1})

    barrier = pltpu.get_barrier_semaphore()

    @pl.when(z > 0)
    def _():
        pl.semaphore_signal(barrier, inc=1, device_id={"head": z - 1}, device_id_type=MESH)

    @pl.when(z < nz - 1)
    def _():
        pl.semaphore_signal(barrier, inc=1, device_id={"head": z + 1}, device_id_type=MESH)

    for r in range(rounds):
        pl.semaphore_signal(barrier, inc=1, device_id={"seq": partner(r)}, device_id_type=MESH)

    @pl.when(first)
    def _():
        r_right[...] = jnp.zeros_like(r_right)

    @pl.when(last)
    def _():
        r_left[...] = jnp.zeros_like(r_left)

    @pl.when(first)
    def _():
        r_back[0] = jnp.zeros(r_back.shape[1:], r_back.dtype)

    @pl.when(last)
    def _():
        r_back[1] = jnp.zeros(r_back.shape[1:], r_back.dtype)

    neighbours = (z > 0).astype(jnp.int32) + (z < nz - 1).astype(jnp.int32)
    pl.semaphore_wait(barrier, rounds + neighbours)

    def block(ref, h):
        return ref[:, pl.ds(pl.multiple_of(h * DK, DK), DK)]

    def states(h):
        return dot(block(k, h), block(v, h), TN), dot(block(q, h), block(o, h), TN)

    def right_stage(c):
        @pl.when(z > 0)
        def _():
            go_right(c).wait_recv()

        for j in range(PIECE):
            h = group + c * PIECE + j
            key_state, grad_state = states(h)
            before_key, before_grad = dec(r_right[c, j]), dec(r_right[c, PIECE + j])
            upto_key, upto_grad = before_key + key_state, before_grad + grad_state
            s_right[c, j] = enc(upto_key)
            s_right[c, PIECE + j] = enc(upto_grad)
            base[0, h] = before_key
            base[1, h] = -upto_grad
        go_right(c).start()

    def left_stage(c):
        @pl.when(z < nz - 1)
        def _():
            go_left(c).wait_recv()

        for j in range(PIECE):
            h = c * PIECE + j
            key_state, grad_state = states(h)
            after_key, after_grad = dec(r_left[c, j]), dec(r_left[c, PIECE + j])
            from_key, from_grad = after_key + key_state, after_grad + grad_state
            s_left[c, j] = enc(from_key)
            s_left[c, PIECE + j] = enc(from_grad)
            base[0, h] = -from_key
            base[1, h] = after_grad
        go_left(c).start()

    def owner_stage(c):
        @pl.when(z > 0)
        def _():
            go_right(c).wait_recv()

        @pl.when(z < nz - 1)
        def _():
            go_left(c).wait_recv()

        for j in range(PIECE):
            h, i = mine * group + c * PIECE + j, c * PIECE + j
            key_state, grad_state = states(h)
            before_key, after_grad = dec(r_right[c, j]), dec(r_left[c, PIECE + j])
            base[0, h] = before_key
            base[1, h] = after_grad
            sums = (
                before_key + key_state + dec(r_left[c, j]),
                dec(r_right[c, PIECE + j]) + grad_state + after_grad,
            )
            for s in range(2):
                own[s, i] = sums[s]
                total[s, i] = sums[s]
                carried[s, i] = jnp.zeros((DK, DK), jnp.float32)
                s_seq[0, c, s * PIECE + j] = enc(sums[s])
        go_seq(0, c).start()

    def seq_stage(r, c):
        go_seq(r - 1, c).wait_recv()
        partner_earlier = later_bit(r - 1).astype(jnp.float32)
        for j in range(PIECE):
            h, i = mine * group + c * PIECE + j, c * PIECE + j
            got_key, got_grad = dec(r_seq[r - 1, c, j]), dec(r_seq[r - 1, c, PIECE + j])
            new_key = carried[0, i] + got_key * partner_earlier
            new_grad = carried[1, i] + got_grad * (1.0 - partner_earlier)
            if r < rounds:
                carried[0, i] = new_key
                carried[1, i] = new_grad
                total_key, total_grad = total[0, i] + got_key, total[1, i] + got_grad
                total[0, i] = total_key
                total[1, i] = total_grad
                s_seq[r, c, j] = enc(total_key)
                s_seq[r, c, PIECE + j] = enc(total_grad)
            else:
                base[0, h] += new_key
                base[1, h] += new_grad
                result[c, j] = enc(jnp.where(first, new_key + own[0, i], new_key))
                result[c, PIECE + j] = enc(jnp.where(first, new_grad, new_grad + own[1, i]))
        if r < rounds:
            go_seq(r, c).start()
        else:
            @pl.when(first)
            def _():
                back_to_right(result.at[c], c).start()

            @pl.when(last)
            def _():
                back_to_left(result.at[c], c).start()

    def relay_left(c):
        back_to_left(r_back.at[1, c], c).wait_recv()

        @pl.when(z > 0)
        def _():
            back_to_left(r_back.at[1, c], c).start()

    def relay_right(c):
        back_to_right(r_back.at[0, c], c).wait_recv()

        @pl.when(z < nz - 1)
        def _():
            back_to_right(r_back.at[0, c], c).start()

    rows = q.shape[0]
    causal = lax.broadcasted_iota(jnp.int32, (rows, rows), 0) >= lax.broadcasted_iota(jnp.int32, (rows, rows), 1)

    def finish(g, c):
        for j in range(PIECE):
            h = g * group + c * PIECE + j
            qh, kh, vh, oh = block(q, h), block(k, h), block(v, h), block(o, h)
            prefix_high, prefix_low = split(base[0, h] + dec(r_back[g, c, j]))
            suffix_high, suffix_low = split(base[1, h] + dec(r_back[g, c, PIECE + j]))
            weights_a = jnp.where(causal, dot(oh, vh, NT), 0.0).astype(jnp.bfloat16)
            weights_b = jnp.where(causal, dot(qh, kh, NT), 0.0).astype(jnp.bfloat16)
            grad_q = dot(weights_a, kh, NN) + dot(oh, prefix_high, NT) + dot(oh, prefix_low, NT)
            grad_k = dot(weights_a, qh, TN) + dot(vh, suffix_high, NT) + dot(vh, suffix_low, NT)
            grad_v = dot(weights_b, oh, TN) + dot(kh, suffix_high, NN) + dot(kh, suffix_low, NN)
            columns = pl.ds(pl.multiple_of(h * DK, DK), DK)
            gq[:, columns] = grad_q.astype(jnp.bfloat16)
            gk[:, columns] = grad_k.astype(jnp.bfloat16)
            gv[:, columns] = grad_v.astype(jnp.bfloat16)

    def valid(c):
        return (c >= 0) & (c < pieces)

    def step(t, carry):
        cl = t - SKEW * (gathered + rounds + nz - 1 - z)

        @pl.when((z < nz - 1) & valid(cl))
        def _():
            relay_left(cl)

        cr = t - SKEW * (gathered + rounds + z)

        @pl.when((z > 0) & valid(cr))
        def _():
            relay_right(cr)

        for r in reversed(range(1, rounds + 1)):
            cs = t - SKEW * (gathered + r)

            @pl.when((first | last) & valid(cs))
            def _():
                seq_stage(r, cs)

        co = t - SKEW * gathered

        @pl.when((first | last) & valid(co))
        def _():
            owner_stage(co)

        c_right, c_left = t - SKEW * z, t - SKEW * (nz - 1 - z)

        @pl.when((z < nz - 1) & valid(c_right))
        def _():
            right_stage(c_right)

        @pl.when((z > 0) & valid(c_left))
        def _():
            left_stage(c_left)

        @pl.when(valid(cr))
        def _():
            finish(0, cr)

        @pl.when(valid(cl))
        def _():
            finish(1, cl)

        return carry

    lax.fori_loop(0, pieces + SKEW * (2 * gathered + rounds), step, 0)

    def drain(c, carry):
        @pl.when(z < nz - 1)
        def _():
            go_right(c).wait_send()
            back_to_right(r_back.at[0, c], c).wait_send()

        @pl.when(z > 0)
        def _():
            go_left(c).wait_send()
            back_to_left(r_back.at[1, c], c).wait_send()

        @pl.when(first | last)
        def _():
            for r in range(rounds):
                go_seq(r, c).wait_send()

        return carry

    lax.fori_loop(0, pieces, drain, 0)


def body(ns, nz, queries, keys, values, grad_out):
    heads = queries.shape[1] // DK
    group = heads // 2
    pieces = group // PIECE
    rounds = ns.bit_length() - 1
    moved = (pieces, 2 * PIECE, DK, DK)

    def bf(*lead):
        return pltpu.VMEM(lead + moved, jnp.bfloat16)

    def f32(count):
        return pltpu.VMEM((2, count, DK, DK), jnp.float32)

    by_piece = pltpu.SemaphoreType.DMA((pieces,))
    by_half = pltpu.SemaphoreType.DMA((2, pieces))
    by_round = pltpu.SemaphoreType.DMA((rounds, pieces))
    return pl.pallas_call(
        functools.partial(kernel, ns, nz),
        out_shape=[jax.ShapeDtypeStruct(queries.shape, jnp.bfloat16)] * 3,
        in_specs=[pl.BlockSpec(memory_space=pltpu.VMEM)] * 4,
        out_specs=[pl.BlockSpec(memory_space=pltpu.VMEM)] * 3,
        scratch_shapes=[
            f32(heads), bf(), bf(), bf(), bf(), f32(group), f32(group), f32(group),
            bf(rounds), bf(rounds), bf(), bf(2),
            by_piece, by_piece, by_piece, by_piece, by_round, by_round, by_half, by_half,
        ],
        compiler_params=pltpu.CompilerParams(
            collective_id=0, has_side_effects=True, vmem_limit_bytes=48 * 1024 * 1024
        ),
    )(queries, keys, values, grad_out)


def solution(mesh):
    ns, nz = mesh.shape["seq"], mesh.shape["head"]
    spec = P(("seq", "head"), None)
    return jax.shard_map(
        functools.partial(body, ns, nz), mesh=mesh, in_specs=(spec,) * 4, out_specs=(spec,) * 3, check_vma=False
    )
```

time: 86.9 us -> 69.8 us (0.80)
  Pallas kernels: 80.7 us -> 63.6 us
    pallas_call x1, Pallas kernels: 80.7 us -> 63.6 us  [body(): pl.pallas_call(functools.partial(kernel, ns, nz), out_shape=[jax.ShapeDty...]
where the time goes in v2:
time: 69.8 us; the launch traced here: 69.6 us
  Pallas kernels  63.6 us (91%)
  local copies, waits for them, and re-layouts  5.35 us (8%)
    pallas_call x1, Pallas kernels, body(): pl.pallas_call(functools.partial(kernel, ns, nz), out_shape=[jax.ShapeDty...  63.6 us
    unnamed x7, local copies, waits for them, and re-layouts  5.35 us

profile of v2, /device:TPU:0, one launch (start us, length us, event | category | flops | bytes accessed | tf_op | source)
XLA Modules:
  0.0 69.6 jit_solution(8934711654026649865)
XLA Ops:
  0.6 0.0 copy-start
  0.6 1.2 %copy-done = bf16[128,4096]{1,0:T(8,128)(2,1)S(1)} copy-done((bf16[128,4096]{1,0:T(8,128)(2,1)S(1)}, bf16[128,4096]{1,0:T(8,128)(2,1)}, u32[]{:S(2)}) %copy-start) | copy-done | bytes 1048600
  1.9 0.0 copy-start.1
  1.9 1.2 %copy-done.1 = bf16[128,4096]{1,0:T(8,128)(2,1)S(1)} copy-done((bf16[128,4096]{1,0:T(8,128)(2,1)S(1)}, bf16[128,4096]{1,0:T(8,128)(2,1)}, u32[]{:S(2)}) %copy-start.1) | copy-done | bytes 1048600
  3.1 63.6 %shard_map.67 = (bf16[128,4096]{1,0:T(8,128)(2,1)S(1)}, bf16[128,4096]{1,0:T(8,128)(2,1)S(1)}, bf16[128,4096]{1,0:T(8,128)(2,1)S(1)}) custom-call(bf16[128,4096]{1,0:T(8,128)(2,1)S(1)} %copy-done, bf16[128,4096]{1,0:T(8,128)(2,1)S(1)} %copy-done.1, bf16[128,4096]{1,0:T(8,128)(2,1)} %v.1, bf16[128,4096]{1,0:T(8,128)(2,1)} %o.1), custom_call_target="tpu_custom_call" | custom-call | tf_op jit(solution)/shard_map/pallas_call | solution.py:326
  66.7 1.0 %copy.10 = bf16[128,4096]{1,0:T(8,128)(2,1)} copy(bf16[128,4096]{1,0:T(8,128)(2,1)S(1)} %get-tuple-element.6) | data formatting | bytes 2097152
  67.7 1.0 %copy.11 = bf16[128,4096]{1,0:T(8,128)(2,1)} copy(bf16[128,4096]{1,0:T(8,128)(2,1)S(1)} %get-tuple-element.7) | data formatting | bytes 2097152
  68.6 1.0 %copy.12 = bf16[128,4096]{1,0:T(8,128)(2,1)} copy(bf16[128,4096]{1,0:T(8,128)(2,1)S(1)} %get-tuple-element.8) | data formatting | bytes 2097152
Async XLA Ops:
  0.6 1.2 %copy-start = (bf16[128,4096]{1,0:T(8,128)(2,1)S(1)}, bf16[128,4096]{1,0:T(8,128)(2,1)}, u32[]{:S(2)}) copy-start(bf16[128,4096]{1,0:T(8,128)(2,1)} %q.1) | copy-start | bytes 3145732
  1.9 1.2 %copy-start.1 = (bf16[128,4096]{1,0:T(8,128)(2,1)S(1)}, bf16[128,4096]{1,0:T(8,128)(2,1)}, u32[]{:S(2)}) copy-start(bf16[128,4096]{1,0:T(8,128)(2,1)} %k.1) | copy-start | bytes 3145732

commit v3 on v2

--- a/solution.py
+++ b/solution.py
@@ -113,13 +113,15 @@
         return dot(block(k, h), block(v, h), TN), dot(block(q, h), block(o, h), TN)
 
     def right_stage(c):
+        fresh = [states(group + c * PIECE + j) for j in range(PIECE)]
+
         @pl.when(z > 0)
         def _():
             go_right(c).wait_recv()
 
         for j in range(PIECE):
             h = group + c * PIECE + j
-            key_state, grad_state = states(h)
+            key_state, grad_state = fresh[j]
             before_key, before_grad = dec(r_right[c, j]), dec(r_right[c, PIECE + j])
             upto_key, upto_grad = before_key + key_state, before_grad + grad_state
             s_right[c, j] = enc(upto_key)
@@ -129,13 +131,15 @@
         go_right(c).start()
 
     def left_stage(c):
+        fresh = [states(c * PIECE + j) for j in range(PIECE)]
+
         @pl.when(z < nz - 1)
         def _():
             go_left(c).wait_recv()
 
         for j in range(PIECE):
             h = c * PIECE + j
-            key_state, grad_state = states(h)
+            key_state, grad_state = fresh[j]
             after_key, after_grad = dec(r_left[c, j]), dec(r_left[c, PIECE + j])
             from_key, from_grad = after_key + key_state, after_grad + grad_state
             s_left[c, j] = enc(from_key)
@@ -145,6 +149,8 @@
         go_left(c).start()
 
     def owner_stage(c):
+        fresh = [states(mine * group + c * PIECE + j) for j in range(PIECE)]
+
         @pl.when(z > 0)
         def _():
             go_right(c).wait_recv()
@@ -155,7 +161,7 @@
 
         for j in range(PIECE):
             h, i = mine * group + c * PIECE + j, c * PIECE + j
-            key_state, grad_state = states(h)
+            key_state, grad_state = fresh[j]
             before_key, after_grad = dec(r_right[c, j]), dec(r_left[c, PIECE + j])
             base[0, h] = before_key
             base[1, h] = after_grad

time: 69.8 us -> 69.7 us (level)
  no operation moved by 1% of the time
where the time goes in v3:
time: 69.7 us; the launch traced here: 69.5 us
  Pallas kernels  63.5 us (91%)
  local copies, waits for them, and re-layouts  5.35 us (8%)
    pallas_call x1, Pallas kernels, body(): pl.pallas_call(functools.partial(kernel, ns, nz), out_shape=[jax.ShapeDty...  63.5 us
    unnamed x7, local copies, waits for them, and re-layouts  5.35 us

profile of v3, /device:TPU:0, one launch (start us, length us, event | category | flops | bytes accessed | tf_op | source)
XLA Modules:
  0.0 69.5 jit_solution(6025555425764727206)
XLA Ops:
  0.6 0.0 copy-start
  0.6 1.2 %copy-done = bf16[128,4096]{1,0:T(8,128)(2,1)S(1)} copy-done((bf16[128,4096]{1,0:T(8,128)(2,1)S(1)}, bf16[128,4096]{1,0:T(8,128)(2,1)}, u32[]{:S(2)}) %copy-start) | copy-done | bytes 1048600
  1.9 0.0 copy-start.1
  1.9 1.2 %copy-done.1 = bf16[128,4096]{1,0:T(8,128)(2,1)S(1)} copy-done((bf16[128,4096]{1,0:T(8,128)(2,1)S(1)}, bf16[128,4096]{1,0:T(8,128)(2,1)}, u32[]{:S(2)}) %copy-start.1) | copy-done | bytes 1048600
  3.1 63.5 %shard_map.67 = (bf16[128,4096]{1,0:T(8,128)(2,1)S(1)}, bf16[128,4096]{1,0:T(8,128)(2,1)S(1)}, bf16[128,4096]{1,0:T(8,128)(2,1)S(1)}) custom-call(bf16[128,4096]{1,0:T(8,128)(2,1)S(1)} %copy-done, bf16[128,4096]{1,0:T(8,128)(2,1)S(1)} %copy-done.1, bf16[128,4096]{1,0:T(8,128)(2,1)} %v.1, bf16[128,4096]{1,0:T(8,128)(2,1)} %o.1), custom_call_target="tpu_custom_call" | custom-call | tf_op jit(solution)/shard_map/pallas_call | solution.py:332
  66.6 1.0 %copy.10 = bf16[128,4096]{1,0:T(8,128)(2,1)} copy(bf16[128,4096]{1,0:T(8,128)(2,1)S(1)} %get-tuple-element.6) | data formatting | bytes 2097152
  67.6 1.0 %copy.11 = bf16[128,4096]{1,0:T(8,128)(2,1)} copy(bf16[128,4096]{1,0:T(8,128)(2,1)S(1)} %get-tuple-element.7) | data formatting | bytes 2097152
  68.5 1.0 %copy.12 = bf16[128,4096]{1,0:T(8,128)(2,1)} copy(bf16[128,4096]{1,0:T(8,128)(2,1)S(1)} %get-tuple-element.8) | data formatting | bytes 2097152
Async XLA Ops:
  0.6 1.2 %copy-start = (bf16[128,4096]{1,0:T(8,128)(2,1)S(1)}, bf16[128,4096]{1,0:T(8,128)(2,1)}, u32[]{:S(2)}) copy-start(bf16[128,4096]{1,0:T(8,128)(2,1)} %q.1) | copy-start | bytes 3145732
  1.9 1.2 %copy-start.1 = (bf16[128,4096]{1,0:T(8,128)(2,1)S(1)}, bf16[128,4096]{1,0:T(8,128)(2,1)}, u32[]{:S(2)}) copy-start(bf16[128,4096]{1,0:T(8,128)(2,1)} %k.1) | copy-start | bytes 3145732
